TPU v7x, 256 devices: a whole 4x4x8 slice. The times are simulated.
256 devices in a mesh: ep: 64 (over z, x, core), etp: 4 (over y).
Axes of the slice: x: 4, y: 4, z: 8, core: 2. Of those that a mesh axis runs over, the one named last changes fastest.
Arguments:
- tokens: bfloat16 [8192, 6144], P('ep', 'etp'), may hold values from -6 to 6
- out_grad: bfloat16 [8192, 6144], P('ep', 'etp'), may hold values from -1.1953125 to 1.1953125
- probs: bfloat16 [8192, 2], P('ep'), may hold values from 0.049804688 to 0.94921875
- expert_ids: int32 [8192, 2], P('ep'), may hold values from 0 to 7, as said below
- slots: int32 [8192, 2], P('ep'), may hold values from -1 to 31, as said below
- counts: int32 [64, 8], P('ep'), may hold values from 0 to 128, as said below
- gate_weight: bfloat16 [6144, 16384], P('etp', 'ep'), may hold values from -0.078125 to 0.078125
- up_weight: bfloat16 [6144, 16384], P('etp', 'ep'), may hold values from -0.078125 to 0.078125
- down_weight: bfloat16 [16384, 6144], P('ep', 'etp'), may hold values from -0.0625 to 0.0625
Outputs:
- token_grad: bfloat16 [8192, 6144], P('ep', 'etp')
- prob_grad: float32 [8192, 2], P('ep')
- gate_grad: bfloat16 [6144, 16384], P('etp', 'ep')
- up_grad: bfloat16 [6144, 16384], P('etp', 'ep')
- down_grad: bfloat16 [16384, 6144], P('ep', 'etp')
Inputs may be any that keep to these rules, and one draw needn't show every extreme that they name: `expert_ids`: each row names two different experts. `slots`: for assignment k of token t of index s of ep: the number of tokens of index s before t that name the same expert, or -1 when that number is 32 or more. counts[s,e] is the number of tokens of index s of ep that name expert e.
All inputs are finite; a program needn't handle non-finite values.
Results may differ from a plain program's by a relative error of at most 0.0058.
Values may be sent and summed in bfloat16 or wider, within the bound.
A program may use at most 128 MiB of HBM per device.

v0:
```python
import jax
import jax.numpy as jnp
from jax import lax
from jax.sharding import PartitionSpec as P

E_WIN = 2
CAP = 32


def backward_rows(summed, weight_p, hidden_cols):
    gate_vals = summed[:, :hidden_cols]
    up_vals = summed[:, hidden_cols : 2 * hidden_cols]
    back_flow = summed[:, 2 * hidden_cols :]
    sigma = jax.nn.sigmoid(gate_vals)
    activation = gate_vals * sigma * up_vals
    scaled = weight_p[:, None]
    weighted = (scaled * activation).astype(jnp.bfloat16)
    gate_diff = scaled * back_flow * up_vals * sigma * (1.0 + gate_vals * (1.0 - sigma))
    up_diff = scaled * back_flow * gate_vals * sigma
    diff_pair = jnp.concatenate([gate_diff, up_diff], 1).astype(jnp.bfloat16)
    prob_part = jnp.sum(activation * back_flow, axis=1).astype(jnp.bfloat16)
    return (diff_pair, weighted, prob_part)


def shards(tokens, out_grad, probs, expert_ids, slots, counts, gate_weight, up_weight, down_weight):
    n_ep = lax.axis_size("ep")
    groups = n_ep // E_WIN
    hidden_cols = gate_weight.shape[1]
    feature_cols = tokens.shape[1]
    slot_rows = E_WIN * CAP
    slots_total = n_ep * CAP
    expert_table = jnp.arange(counts.shape[1], dtype=jnp.int32)
    limit = jnp.sum(
        jnp.where(
            expert_ids[:, :, None] == expert_table[None, None, :], counts[0][None, None, :], 0
        ),
        axis=2,
    )
    usable = (expert_ids < E_WIN) & (slots >= 0) & (slots < jnp.minimum(limit, CAP))
    target = jnp.where(usable, expert_ids * CAP + slots, -1)
    pick_map = (jnp.arange(slot_rows, dtype=jnp.int32)[:, None, None] == target[None, :, :]).astype(
        jnp.float32
    )
    selector = jnp.sum(pick_map, axis=2)
    select_half = selector.astype(jnp.bfloat16)
    x_rows = jnp.dot(select_half, tokens, preferred_element_type=jnp.float32).astype(jnp.bfloat16)
    dy_rows = jnp.dot(select_half, out_grad, preferred_element_type=jnp.float32).astype(
        jnp.bfloat16
    )
    p_rows = jnp.einsum(
        "rtk,tk->r", pick_map, probs.astype(jnp.float32), precision=lax.Precision.HIGHEST
    ).astype(jnp.bfloat16)
    x_blocks = x_rows.reshape(E_WIN, CAP, feature_cols)
    dy_blocks = dy_rows.reshape(E_WIN, CAP, feature_cols)
    p_blocks = p_rows.reshape(E_WIN, CAP)
    x_send = jnp.repeat(x_blocks, groups, axis=0)
    dy_send = jnp.repeat(dy_blocks, groups, axis=0)
    p_send = jnp.repeat(p_blocks, groups, axis=0)
    x_all, dy_all, p_all = (
        lax.all_to_all(x_send, "ep", split_axis=0, concat_axis=0, tiled=True),
        lax.all_to_all(dy_send, "ep", split_axis=0, concat_axis=0, tiled=True),
        lax.all_to_all(p_send, "ep", split_axis=0, concat_axis=0, tiled=True),
    )
    x_slot = x_all.reshape(slots_total, feature_cols)
    dy_slot = dy_all.reshape(slots_total, feature_cols)
    p_slot = p_all.reshape(slots_total).astype(jnp.float32)
    w_pair = jnp.concatenate([gate_weight, up_weight], 1)
    forward = jnp.dot(x_slot, w_pair, preferred_element_type=jnp.float32)
    backward = lax.dot_general(
        dy_slot, down_weight, (((1,), (1,)), ((), ())), preferred_element_type=jnp.float32
    )
    summed = lax.psum(jnp.concatenate([forward, backward], 1), "etp")
    diff_pair, weighted, prob_part = backward_rows(summed, p_slot, hidden_cols)
    pair_grad = lax.dot_general(
        x_slot, diff_pair, (((0,), (0,)), ((), ())), preferred_element_type=jnp.float32
    )
    gate_grad = pair_grad[:, :hidden_cols].astype(jnp.bfloat16)
    up_grad = pair_grad[:, hidden_cols:].astype(jnp.bfloat16)
    down_grad = lax.dot_general(
        weighted, dy_slot, (((0,), (0,)), ((), ())), preferred_element_type=jnp.float32
    ).astype(jnp.bfloat16)
    slot_part = lax.dot_general(
        diff_pair, w_pair, (((1,), (1,)), ((), ())), preferred_element_type=jnp.float32
    ).astype(jnp.bfloat16)
    back_x, back_p = (
        lax.all_to_all(
            slot_part.reshape(n_ep, CAP, feature_cols),
            "ep",
            split_axis=0,
            concat_axis=0,
            tiled=True,
        ),
        lax.all_to_all(prob_part.reshape(n_ep, CAP), "ep", split_axis=0, concat_axis=0, tiled=True),
    )
    summed_x = jnp.sum(
        back_x.reshape(E_WIN, groups, CAP, feature_cols).astype(jnp.float32), axis=1
    ).reshape(slot_rows, feature_cols)
    summed_p = jnp.sum(back_p.reshape(E_WIN, groups, CAP).astype(jnp.float32), axis=1).reshape(
        slot_rows
    )
    token_grad = lax.dot_general(
        selector,
        summed_x,
        (((0,), (0,)), ((), ())),
        precision=lax.Precision.HIGHEST,
        preferred_element_type=jnp.float32,
    ).astype(jnp.bfloat16)
    prob_grad = jnp.einsum("rtk,r->tk", pick_map, summed_p, precision=lax.Precision.HIGHEST)
    return (token_grad, prob_grad, gate_grad, up_grad, down_grad)


def solution(mesh):
    in_specs = (
        P("ep", "etp"),
        P("ep", "etp"),
        P("ep", None),
        P("ep", None),
        P("ep", None),
        P("ep", None),
        P("etp", "ep"),
        P("etp", "ep"),
        P("ep", "etp"),
    )
    out_specs = (P("ep", "etp"), P("ep", None), P("etp", "ep"), P("etp", "ep"), P("ep", "etp"))
    return jax.shard_map(shards, mesh=mesh, in_specs=in_specs, out_specs=out_specs, check_vma=False)
```

profile of v0, /device:TPU:6, one launch (start us, length us, event | category | flops | bytes accessed | tf_op | source)
XLA Modules:
  0.0 640.3 jit_solution(5596827705233082045)
XLA Ops:
  7.2 0.9 select_reduce_fusion
  8.0 0.7 and_select_fusion
  8.7 1.2 convolution_convert_fusion.5
  9.9 3.4 broadcast_in_dim.37
  13.4 12.3 %all-to-all-start.1 = ((bf16[64,32,1536]{2,1,0:T(8,128)(2,1)}), bf16[64,32,1536]{2,1,0:T(8,128)(2,1)}, u32[]{:S(2)}, u32[]{:S(2)}) async-start(bf16[64,32,1536]{2,1,0:T(8,128)(2,1)} %bitcast.38), calls=%async_computation.1 | async-start | bytes 12582912 | tf_op jit(solution)/shard_map/all_to_all | solution.py:60
  25.7 0.2 convolution_convert_fusion.4
  25.9 141.1 %all-to-all-done.1 = bf16[64,32,1536]{2,1,0:T(8,128)(2,1)} async-done(((bf16[64,32,1536]{2,1,0:T(8,128)(2,1)}), bf16[64,32,1536]{2,1,0:T(8,128)(2,1)}, u32[]{:S(2)}, u32[]{:S(2)}) %all-to-all-start.1) | async-done | bytes 6291488 | tf_op jit(solution)/shard_map/all_to_all | solution.py:60
  166.9 3.4 broadcast_in_dim.38
  170.3 5.9 all-to-all-start.2
  176.3 1.0 copy-done.4
  177.4 1.2 copy-done.5
  178.6 7.8 %fusion.13 = f32[2048,512]{0,1:T(8,128)} fusion(bf16[2048,1536]{1,0:T(8,128)(2,1)} %bitcast.5, bf16[1536,512]{1,0:T(8,128)(2,1)S(1)} %constant_dynamic-update-slice_fusion), kind=kOutput, calls=%fused_computation.38 | convolution fusion | flops 3221225472 | bytes 12058624 | tf_op jit(solution)/shard_map/dot_general | solution.py:68
  186.4 131.1 %all-to-all-done.2 = bf16[64,32,1536]{2,1,0:T(8,128)(2,1)} async-done(((bf16[64,32,1536]{2,1,0:T(8,128)(2,1)}), bf16[64,32,1536]{2,1,0:T(8,128)(2,1)}, u32[]{:S(2)}, u32[]{:S(2)}) %all-to-all-start.2) | async-done | bytes 6291488 | tf_op jit(solution)/shard_map/all_to_all | solution.py:61
  317.4 4.7 fusion.14
  322.2 3.0 pad_maximum_fusion
  325.2 0.6 copy-done.7
  325.9 0.1 fusion
  326.5 13.2 %all_to_all.30 = bf16[64,1,32]{2,1,0:T(2,128)(2,1)S(1)} all-to-all(bf16[64,1,32]{2,1,0:T(2,128)(2,1)S(1)} %copy.27), channel_id=1, replica_groups=mesh['ep'=64,'etp'=4] {'ep'}, dimensions={0} | all-to-all | bytes 8192 | tf_op jit(solution)/shard_map/all_to_all | solution.py:62
  339.9 114.0 %all-reduce.2.cloned.1.call-done = f32[2048,768]{0,1:T(8,128)} async-done(((f32[2048,768]{0,1:T(8,128)}), f32[2048,768]{0,1:T(8,128)}) %all-reduce.2.cloned.1.call-update) | async-done | bytes 6291472 | tf_op jit(solution)/shard_map/psum | solution.py:72
  454.0 4.3 multiply_convert_fusion.2
  458.2 0.7 convert_element_type.90
  458.9 10.5 %all-to-all-start.4 = ((bf16[64,1,32]{2,1,0:T(2,128)(2,1)}), bf16[64,1,32]{2,1,0:T(2,128)(2,1)S(1)}, u32[]{:S(2)}, u32[]{:S(2)}) async-start(bf16[64,1,32]{2,1,0:T(2,128)(2,1)} %convert_element_type.90), calls=%async_computation.4 | async-start | bytes 65536 | tf_op jit(solution)/shard_map/all_to_all | solution.py:93
  469.5 6.8 %convolution_convert_fusion = bf16[2048,1536]{1,0:T(8,128)(2,1)} fusion(bf16[1536,512]{1,0:T(8,128)(2,1)} %copy-done.5, bf16[2048,256]{0,1:T(8,128)(2,1)S(1)} %get-tuple-element.6, bf16[2048,256]{0,1:T(8,128)(2,1)S(1)} %get-tuple-element.5), kind=kOutput, calls=%fused_computation.1 | convolution fusion | flops 3228565504 | bytes 9961472 | tf_op jit(solution)/shard_map/dot_general | solution.py:82
  476.3 1.0 all-to-all-done.4
  477.3 9.5 %all-to-all-start.3 = ((bf16[64,32,1536]{2,1,0:T(8,128)(2,1)}), bf16[64,32,1536]{2,1,0:T(8,128)(2,1)}, u32[]{:S(2)}, u32[]{:S(2)}) async-start(bf16[64,32,1536]{2,1,0:T(8,128)(2,1)} %bitcast.39), calls=%async_computation.3 | async-start | bytes 12582912 | tf_op jit(solution)/shard_map/all_to_all | solution.py:86
  486.8 6.3 convolution_convert_fusion.1
  493.0 1.2 fusion.12
  494.3 6.8 %convolution_convert_fusion.2 = bf16[256,1536]{1,0:T(8,128)(2,1)} fusion(bf16[2048,1536]{1,0:T(8,128)(2,1)} %bitcast.8, f32[2048]{0:T(1024)S(1)} %reshape.88, f32[2048,768]{0,1:T(8,128)} %all-reduce.2.cloned.1.call-done), kind=kOutput, calls=%fused_computation.4 | convolution fusion | flops 1614675968 | bytes 11280384 | tf_op jit(solution)/shard_map/dot_general | solution.py:79
  501.2 0.7 fusion.3
  501.9 126.2 %all-to-all-done.3 = bf16[64,32,1536]{2,1,0:T(8,128)(2,1)} async-done(((bf16[64,32,1536]{2,1,0:T(8,128)(2,1)}), bf16[64,32,1536]{2,1,0:T(8,128)(2,1)}, u32[]{:S(2)}, u32[]{:S(2)}) %all-to-all-start.3) | async-done | bytes 6291488 | tf_op jit(solution)/shard_map/all_to_all | solution.py:86
  628.0 3.9 convert_reduce_fusion
  631.9 1.6 convolution_convert_fusion.3
  (28 shorter events, 1.0 us)
Async XLA Ops:
  7.2 310.3 %copy-start = (bf16[256,1536]{1,0:T(8,128)(2,1)S(1)}, bf16[256,1536]{1,0:T(8,128)(2,1)}, u32[]{:S(2)}) copy-start(bf16[256,1536]{1,0:T(8,128)(2,1)} %param.17) | copy-start | bytes 2359300
  13.4 12.3 %copy-start.6 = (bf16[128,1536]{1,0:T(8,128)(2,1)S(1)}, bf16[128,1536]{1,0:T(8,128)(2,1)}, u32[]{:S(2)}) copy-start(bf16[128,1536]{1,0:T(8,128)(2,1)} %param.10) | copy-start | bytes 1179652
  13.4 153.5 %all-to-all-start.1 = ((bf16[64,32,1536]{2,1,0:T(8,128)(2,1)}), bf16[64,32,1536]{2,1,0:T(8,128)(2,1)}, u32[]{:S(2)}, u32[]{:S(2)}) async-start(bf16[64,32,1536]{2,1,0:T(8,128)(2,1)} %bitcast.38), calls=%async_computation.1 | async-start | bytes 12582912 | tf_op jit(solution)/shard_map/all_to_all | solution.py:60
  170.3 5.9 copy-start.3
  170.3 147.1 %all-to-all-start.2 = ((bf16[64,32,1536]{2,1,0:T(8,128)(2,1)}), bf16[64,32,1536]{2,1,0:T(8,128)(2,1)}, u32[]{:S(2)}, u32[]{:S(2)}) async-start(bf16[64,32,1536]{2,1,0:T(8,128)(2,1)} %bitcast.37), calls=%async_computation.2 | async-start | bytes 12582912 | tf_op jit(solution)/shard_map/all_to_all | solution.py:61
  176.2 1.1 copy-start.4
  176.2 277.8 %all-reduce.2.cloned.1.call-start = ((), (), s32[]{:S(2)}) async-start(), calls=%async_computation.5 | async-start | bytes 12582912 | tf_op jit(solution)/shard_map/psum | solution.py:72
  177.4 1.2 copy-start.5
  317.4 4.8 copy-start.2
  325.2 0.7 copy-start.7
  458.9 18.3 %all-to-all-start.4 = ((bf16[64,1,32]{2,1,0:T(2,128)(2,1)}), bf16[64,1,32]{2,1,0:T(2,128)(2,1)S(1)}, u32[]{:S(2)}, u32[]{:S(2)}) async-start(bf16[64,1,32]{2,1,0:T(2,128)(2,1)} %convert_element_type.90), calls=%async_computation.4 | async-start | bytes 65536 | tf_op jit(solution)/shard_map/all_to_all | solution.py:93
  477.3 150.8 %all-to-all-start.3 = ((bf16[64,32,1536]{2,1,0:T(8,128)(2,1)}), bf16[64,32,1536]{2,1,0:T(8,128)(2,1)}, u32[]{:S(2)}, u32[]{:S(2)}) async-start(bf16[64,32,1536]{2,1,0:T(8,128)(2,1)} %bitcast.39), calls=%async_computation.3 | async-start | bytes 12582912 | tf_op jit(solution)/shard_map/all_to_all | solution.py:86
  501.2 132.3 %copy-start.1 = (bf16[256,1536]{1,0:T(8,128)(2,1)S(1)}, bf16[256,1536]{1,0:T(8,128)(2,1)}, u32[]{:S(2)}) copy-start(bf16[256,1536]{1,0:T(8,128)(2,1)} %param.17) | copy-start | bytes 2359300
Sparse Core Ops, SparseCore 0:
  325.4 128.5 all-reduce.1
where the time goes:
time: 641 us; the launch traced here: 640 us
  waiting for transfers between devices  513 us (80%)
  starting transfers between devices  38.2 us (6%)
  matrix products  36.2 us (6%)
  between operations  14.2 us (2%)
  blocking collectives  13.2 us (2%)
  other arithmetic  12.8 us (2%)
  local copies, waits for them, and re-layouts  12.4 us (2%)
    all_to_all x1, waiting for transfers between devices, shards(): lax.all_to_all(x_send, 'ep', split_axis=0, concat_axis=0, tiled=True)  141 us
    all_to_all x1, waiting for transfers between devices, shards(): lax.all_to_all(dy_send, 'ep', split_axis=0, concat_axis=0, tiled=True)  131 us
    all_to_all x1, waiting for transfers between devices, shards(): lax.all_to_all(slot_part.reshape(n_ep, CAP, feature_cols), 'ep', split_ax...  126 us
    psum x1, waiting for transfers between devices, shards(): summed = lax.psum(jnp.concatenate([forward, backward], 1), 'etp')  114 us
    all_to_all x1, blocking collectives, shards(): lax.all_to_all(p_send, 'ep', split_axis=0, concat_axis=0, tiled=True)  13.2 us
  transfers between devices with their start and end apart: 5, of which 5 were waited for; matrix products, arithmetic and copies ran while one was open for 5% of the time, Pallas kernels for 0%

commit v1 on v0

v1 whole, which is shorter than its diff:
```python
import jax
import jax.numpy as jnp
from jax import lax
from jax.experimental import pallas as pl
from jax.experimental.pallas import tpu as pltpu
from jax.sharding import PartitionSpec as P

E_WIN = 2
CAP = 32
BF = jnp.bfloat16
F32 = jnp.float32
NT = (((1,), (1,)), ((), ()))
TN = (((0,), (0,)), ((), ()))
ORDER = (
    (0, 1, 7, 2, 6, 3, 4, 5),
    (0, 1, 7, 2, 6, 3, 5, 4),
    (0, 7, 1, 6, 2, 5, 3, 4),
    (0, 7, 1, 6, 2, 5, 4, 3),
)
PROB = 128


def moe_kernel(
    xin, wg_hbm, wu_hbm, wd_hbm,
    out, gate_out, up_out, down_out,
    wg, wu, wd, xy, part, rss, rsr, diff, sp, r1r, sums, r2s, r2r, r3s, r3r, acc_pair, acc_down,
    w_sem, own_sem,
    zs_dn, zs_up, zs_other, z_recv, xs_up, xs_dn, x_recv, xf_send, x2_recv, sib_send, sib_recv,
    rs_send, rs_recv, ag_send, ag_recv, r1_send, r1_recv, r2_send, r2_recv, r3_send, r3_recv,
):
    feat = xin.shape[-1]
    hid = wg.shape[1]
    ep = lax.axis_index("ep")
    y = lax.axis_index("etp")
    core = lax.rem(ep, 2)
    x = lax.rem(ep // 2, 4)
    z = ep // 8
    zl = lax.rem(z, 4)
    group = z // 4

    def at(zz, xx, cc, yy):
        return ((zz * 4 + xx) * 2 + cc, yy)

    def z_dev(shift):
        return at(lax.rem(z + shift, 8), x, core, y)

    x_up = at(z, lax.rem(x + 1, 4), core, y)
    x_dn = at(z, lax.rem(x + 3, 4), core, y)
    sibling = at(z, x, 1 - core, y)
    q_up = lax.rem(y + 1, 4)
    q_dn = lax.rem(y + 3, 4)
    q_op = lax.rem(y + 2, 4)
    y_up = (ep, q_up)
    y_dn = (ep, q_dn)

    sends = []

    def remote(src, dst, send_sem, recv_sem, dev):
        return pltpu.make_async_remote_copy(
            src_ref=src, dst_ref=dst, send_sem=send_sem, recv_sem=recv_sem,
            device_id=dev, device_id_type=pl.DeviceIdType.MESH,
        )

    def push(src, dst, send_sem, recv_sem, dev):
        copy = remote(src, dst, send_sem, recv_sem, dev)
        copy.start()
        sends.append((None, copy))

    def arrive(dst, recv_sem):
        remote(dst, dst, own_sem, recv_sem, sibling).wait_recv()

    barrier = pltpu.get_barrier_semaphore()
    partners = [z_dev(s) for s in range(1, 8)] + [x_up, x_dn, y_up, y_dn, sibling]
    for dev in partners:
        pl.semaphore_signal(barrier, inc=1, device_id=dev, device_id_type=pl.DeviceIdType.MESH)
    w_copies = [
        pltpu.make_async_copy(src, dst, w_sem.at[i])
        for i, (src, dst) in enumerate(((wg_hbm, wg), (wu_hbm, wu), (wd_hbm, wd)))
    ]
    for copy in w_copies:
        copy.start()
    xy[:, 0, 0, 0] = xin[group]
    pl.semaphore_wait(barrier, len(partners))

    def z_branch(v, k):
        r = ORDER[v][k]
        src = xy.at[:, k, 0, 0]
        down = r <= 5 - v
        todo = []
        if (down or r == 0) and v > 0:
            to = ORDER[v - 1].index(r + 1)
            todo.append(
                lambda: remote(src, xy.at[:, to, 0, 0], zs_dn.at[k], z_recv.at[to], z_dev(7))
            )
        if (not down or r == 0) and v < 3:
            back_to = ORDER[v + 1].index((r + 7) % 8)
            todo.append(
                lambda: remote(src, xy.at[:, back_to, 0, 0], zs_up.at[k], z_recv.at[back_to], z_dev(1))
            )
        if k == 0:
            if v <= 1:
                w, far, shift = 3, v + 1, 7 - v
            else:
                w, far, shift = 0, 8 - (4 - v), 4 - v
            slot = ORDER[w].index(far)
            todo.append(
                lambda: remote(
                    xin.at[1 - group], xy.at[:, slot, 0, 0], zs_other, z_recv.at[slot], z_dev(shift)
                )
            )
        return todo

    def z_step(k):
        if k > 0:
            arrive(xy.at[:, k, 0, 0], z_recv.at[k])
        for v in range(4):
            todo = z_branch(v, k)
            if todo:
                def run(todo=todo):
                    for make in todo:
                        make().start()

                pl.when(zl == v)(run)
                sends.append((v, todo))
        src = xy.at[:, k, 0, 0]
        push(src, xy.at[:, k, 0, 1], xs_up.at[k], x_recv.at[0, k], x_up)
        push(src, xy.at[:, k, 0, 2], xs_dn.at[k], x_recv.at[1, k], x_dn)

    def x_step(k):
        arrive(xy.at[:, k, 0, 1], x_recv.at[0, k])
        if k % 2 == 0:
            push(xy.at[:, k, 0, 1], xy.at[:, k, 0, 3], xf_send.at[k], x2_recv.at[k], x_up)
        arrive(xy.at[:, k, 0, 2], x_recv.at[1, k])
        if k % 2 == 1:
            push(xy.at[:, k, 0, 2], xy.at[:, k, 0, 3], xf_send.at[k], x2_recv.at[k], x_dn)

    def sib_step(k):
        arrive(xy.at[:, k, 0, 3], x2_recv.at[k])
        push(xy.at[:, k, 0], xy.at[:, k, 1], sib_send.at[k], sib_recv.at[k], sibling)

    def sib_wait(k):
        arrive(xy.at[:, k, 1], sib_recv.at[k])

    def partial_sums(j):
        if j == 0:
            for copy in w_copies:
                copy.wait()

        def body(p, carry):
            xs = xy[0, 2 * j + p].reshape(8 * CAP, feat)
            dys = xy[1, 2 * j + p].reshape(8 * CAP, feat)
            rows = pl.ds(2 * p, 2)
            b = j % 2
            part[b, rows, :, 0:hid] = jnp.dot(
                xs, wg[...], preferred_element_type=F32).reshape(2, 4 * CAP, hid)
            part[b, rows, :, hid:2 * hid] = jnp.dot(
                xs, wu[...], preferred_element_type=F32).reshape(2, 4 * CAP, hid)
            part[b, rows, :, 2 * hid:3 * hid] = lax.dot_general(
                dys, wd[...], NT, preferred_element_type=F32).reshape(2, 4 * CAP, hid)
            return carry

        lax.fori_loop(0, 2, body, 0)

    LO, HI = slice(0, 64), slice(64, 128)

    def rs_a(j):
        b = j % 2
        for slot, (q, half, dev) in enumerate(
            ((q_op, LO, y_up), (q_op, HI, y_dn), (q_up, HI, y_up), (q_dn, LO, y_dn))
        ):
            rss[j, slot] = part[b, q, half].astype(BF)
            push(rss.at[j, slot], rsr.at[j, slot], rs_send.at[j, slot], rs_recv.at[j, slot], dev)

    def rs_b(j):
        b = j % 2
        for slot, (q, half, dev) in ((4, (q_up, LO, y_up)), (5, (q_dn, HI, y_dn))):
            arrive(rsr.at[j, slot - 4], rs_recv.at[j, slot - 4])
            rss[j, slot] = (part[b, q, half] + rsr[j, slot - 4].astype(F32)).astype(BF)
            push(rss.at[j, slot], rsr.at[j, slot], rs_send.at[j, slot], rs_recv.at[j, slot], dev)

    def rs_c(j):
        b = j % 2
        for slot in range(2, 6):
            arrive(rsr.at[j, slot], rs_recv.at[j, slot])
        for half, one, two in ((LO, 4, 3), (HI, 2, 5)):
            total = part[b, y, half] + rsr[j, one].astype(F32) + rsr[j, two].astype(F32)
            gate = total[:, 0:hid]
            up = total[:, hid:2 * hid]
            back = total[:, 2 * hid:3 * hid]
            sg = jax.nn.sigmoid(gate)
            silu = gate * sg
            act = silu * up
            diff[j, y, half, 0:hid] = (back * up * sg * (1.0 + gate * (1.0 - sg))).astype(BF)
            diff[j, y, half, hid:2 * hid] = (back * silu).astype(BF)
            diff[j, y, half, 2 * hid:3 * hid] = act.astype(BF)
            prob = act * back
            lanes = prob[:, 0:PROB]
            for i in range(1, hid // PROB):
                lanes = lanes + prob[:, i * PROB:(i + 1) * PROB]
            diff[j, y, half, 3 * hid:] = lanes.astype(BF)
        for i, half in enumerate((LO, HI)):
            src = diff.at[j, y, half]
            push(src, src, ag_send.at[j, i], ag_recv.at[j, i], y_up)
            push(src, src, ag_send.at[j, 2 + i], ag_recv.at[j, 2 + i], y_dn)

    def ag_b(j):
        lo = diff.at[j, q_dn, LO]
        arrive(lo, ag_recv.at[j, 0])
        push(lo, lo, ag_send.at[j, 4], ag_recv.at[j, 4], y_up)
        hi = diff.at[j, q_up, HI]
        arrive(hi, ag_recv.at[j, 3])
        push(hi, hi, ag_send.at[j, 5], ag_recv.at[j, 5], y_dn)

    def ag_c(j):
        arrive(diff.at[j, q_dn, HI], ag_recv.at[j, 1])
        arrive(diff.at[j, q_up, LO], ag_recv.at[j, 2])
        arrive(diff.at[j, q_op, LO], ag_recv.at[j, 4])
        arrive(diff.at[j, q_op, HI], ag_recv.at[j, 5])

    def slot_rows(j):
        def rows_of(p, side):
            d = diff[j, 2 * p + side]
            value = lax.dot_general(d[:, 0:hid], wg[...], NT, preferred_element_type=F32)
            value = value + lax.dot_general(
                d[:, hid:2 * hid], wu[...], NT, preferred_element_type=F32)
            return value, d[:, 3 * hid:]

        def theirs(p, carry):
            value, prob = rows_of(p, 1)
            sp[j, p, :, 0:feat] = value.astype(BF)
            sp[j, p, :, feat:] = prob
            return carry

        def mine(p, carry):
            value, prob = rows_of(p, 0)
            sums[j % 2, p, :, 0:feat] = value
            sums[j % 2, p, :, feat:] = prob.astype(F32)
            return carry

        lax.fori_loop(0, 2, theirs, 0)
        push(sp.at[j], r1r.at[j], r1_send.at[j], r1_recv.at[j], sibling)
        lax.fori_loop(0, 2, mine, 0)

    def rel(i):
        return slice(i * CAP, (i + 1) * CAP)

    def r2_a(j):
        b = j % 2
        arrive(r1r.at[j], r1_recv.at[j])
        sums[b] = sums[b] + r1r[j].astype(F32)
        for slot, (p, i, dev) in enumerate(
            ((0, 3, x_up), (1, 3, x_dn), (1, 2, x_up), (0, 1, x_dn))
        ):
            r2s[j, slot] = sums[b, p, rel(i)].astype(BF)
            push(r2s.at[j, slot], r2r.at[j, slot], r2_send.at[j, slot], r2_recv.at[j, slot], dev)

    def r2_b(j):
        b = j % 2
        for slot, (p, i, dev) in ((4, (0, 2, x_up)), (5, (1, 1, x_dn))):
            arrive(r2r.at[j, slot - 4], r2_recv.at[j, slot - 4])
            r2s[j, slot] = (sums[b, p, rel(i)] + r2r[j, slot - 4].astype(F32)).astype(BF)
            push(r2s.at[j, slot], r2r.at[j, slot], r2_send.at[j, slot], r2_recv.at[j, slot], dev)

    def r2_c(j):
        b = j % 2
        for slot in range(2, 6):
            arrive(r2r.at[j, slot], r2_recv.at[j, slot])
        for p, one, two in ((0, 4, 3), (1, 2, 5)):
            k = 2 * j + p
            total = sums[b, p, rel(0)] + r2r[j, one].astype(F32) + r2r[j, two].astype(F32)
            if k == 0:
                r3r[0] = total.astype(BF)
                continue
            r3s[k] = total.astype(BF)
            for v in range(4):
                r = ORDER[v][k]
                s = 8 - r
                todo = [lambda r=r, s=s, k=k: remote(
                    r3s.at[k], r3r.at[s], r3_send.at[k], r3_recv.at[s], z_dev(r))]

                def run(todo=todo):
                    for make in todo:
                        make().start()

                pl.when(zl == v)(run)
                sends.append((v, todo))

    tile = 256

    def grads(j):
        def pair_body(t, carry):
            cols = pl.ds(pl.multiple_of(t * tile, tile), tile)
            xs = xy[0, 2 * j:2 * j + 2, :, :, :, cols].reshape(16 * CAP, tile)
            d = diff[j, :, :, 0:2 * hid].reshape(16 * CAP, 2 * hid)
            new = lax.dot_general(xs, d, TN, preferred_element_type=F32)
            if j == 0:
                acc_pair[cols, :] = new
            elif j < 3:
                acc_pair[cols, :] += new
            else:
                new = new + acc_pair[cols, :]
                gate_out[cols, :] = new[:, 0:hid].astype(BF)
                up_out[cols, :] = new[:, hid:].astype(BF)
            return carry

        def down_body(t, carry):
            cols = pl.ds(pl.multiple_of(t * tile, tile), tile)
            dys = xy[1, 2 * j:2 * j + 2, :, :, :, cols].reshape(16 * CAP, tile)
            act = diff[j, :, :, 2 * hid:3 * hid].reshape(16 * CAP, hid)
            new = lax.dot_general(act, dys, TN, preferred_element_type=F32)
            if j == 0:
                acc_down[:, cols] = new
            elif j < 3:
                acc_down[:, cols] += new
            else:
                down_out[:, cols] = (new + acc_down[:, cols]).astype(BF)
            return carry

        lax.fori_loop(0, feat // tile, pair_body, 0)
        lax.fori_loop(0, feat // tile, down_body, 0)

    for tick in range(19):
        if tick < 8:
            z_step(tick)
        if 0 <= tick - 1 < 8:
            x_step(tick - 1)
        if 0 <= tick - 2 < 8:
            sib_step(tick - 2)
        for lag, stage in (
            (5, rs_b), (6, rs_c), (7, ag_b), (9, r2_a), (10, r2_b), (11, r2_c)
        ):
            j, odd = divmod(tick - lag, 2)
            if odd == 0 and 0 <= j < 4:
                stage(j)
        if 0 <= tick - 3 < 8:
            sib_wait(tick - 3)
        j, odd = divmod(tick - 4, 2)
        if odd == 0 and 0 <= j < 4:
            partial_sums(j)
            rs_a(j)
        j, odd = divmod(tick - 8, 2)
        if odd == 0 and 0 <= j < 4:
            ag_c(j)
            slot_rows(j)
        j, odd = divmod(tick - 9, 2)
        if odd == 0 and 0 <= j < 4:
            grads(j)

    out[...] = jnp.zeros_like(out)
    for s in range(8):
        if s > 0:
            arrive(r3r.at[s], r3_recv.at[s])
        owner = lax.rem(z + s, 8) // 4
        out[owner] = out[owner] + r3r[s].astype(F32)
    for v, item in sends:
        if v is None:
            item.wait_send()
        else:
            def run(item=item):
                for make in item:
                    make().wait_send()

            pl.when(zl == v)(run)


def moe(xin, gate_weight, up_weight, down_weight):
    feat, hid = gate_weight.shape
    width = 3 * hid + PROB
    wide = feat + PROB
    dma = pltpu.SemaphoreType.DMA
    vmem = pl.BlockSpec(memory_space=pltpu.VMEM)
    hbm = pl.BlockSpec(memory_space=pl.ANY)
    return pl.pallas_call(
        moe_kernel,
        out_shape=(
            jax.ShapeDtypeStruct((E_WIN, CAP, wide), F32),
            jax.ShapeDtypeStruct((feat, hid), BF),
            jax.ShapeDtypeStruct((feat, hid), BF),
            jax.ShapeDtypeStruct((hid, feat), BF),
        ),
        in_specs=[vmem, hbm, hbm, hbm],
        out_specs=(vmem, vmem, vmem, vmem),
        scratch_shapes=[
            pltpu.VMEM((feat, hid), BF),
            pltpu.VMEM((feat, hid), BF),
            pltpu.VMEM((hid, feat), BF),
            pltpu.VMEM((2, 8, 2, 4, CAP, feat), BF),
            pltpu.VMEM((2, 4, 4 * CAP, 3 * hid), F32),
            pltpu.VMEM((4, 6, 2 * CAP, 3 * hid), BF),
            pltpu.VMEM((4, 6, 2 * CAP, 3 * hid), BF),
            pltpu.VMEM((4, 4, 4 * CAP, width), BF),
            pltpu.VMEM((4, 2, 4 * CAP, wide), BF),
            pltpu.VMEM((4, 2, 4 * CAP, wide), BF),
            pltpu.VMEM((2, 2, 4 * CAP, wide), F32),
            pltpu.VMEM((4, 6, CAP, wide), BF),
            pltpu.VMEM((4, 6, CAP, wide), BF),
            pltpu.VMEM((8, CAP, wide), BF),
            pltpu.VMEM((8, CAP, wide), BF),
            pltpu.VMEM((feat, 2 * hid), F32),
            pltpu.VMEM((hid, feat), F32),
            dma((3,)), dma,
            dma((8,)), dma((8,)), dma, dma((8,)),
            dma((8,)), dma((8,)), dma((2, 8)), dma((8,)), dma((8,)), dma((8,)), dma((8,)),
            dma((4, 6)), dma((4, 6)), dma((4, 6)), dma((4, 6)),
            dma((4,)), dma((4,)), dma((4, 6)), dma((4, 6)), dma((8,)), dma((8,)),
        ],
        compiler_params=pltpu.CompilerParams(
            collective_id=0, has_side_effects=True, vmem_limit_bytes=62 * 1024 * 1024
        ),
        cost_estimate=pl.CostEstimate(
            flops=13 * 10**9, bytes_accessed=8 * 10**6, transcendentals=0
        ),
    )(xin, gate_weight, up_weight, down_weight)


def shards(tokens, out_grad, probs, expert_ids, slots, counts, gate_weight, up_weight, down_weight):
    feature_cols = tokens.shape[1]
    slot_rows = E_WIN * CAP
    expert_table = jnp.arange(counts.shape[1], dtype=jnp.int32)
    limit = jnp.sum(
        jnp.where(
            expert_ids[:, :, None] == expert_table[None, None, :], counts[0][None, None, :], 0
        ),
        axis=2,
    )
    usable = (expert_ids < E_WIN) & (slots >= 0) & (slots < jnp.minimum(limit, CAP))
    target = jnp.where(usable, expert_ids * CAP + slots, -1)
    pick_map = jnp.arange(slot_rows, dtype=jnp.int32)[:, None, None] == target[None, :, :]
    selector = jnp.sum(pick_map.astype(F32), axis=2)
    scaled = jnp.sum(jnp.where(pick_map, probs.astype(F32)[None], 0.0), axis=2)
    x_rows = jnp.dot(selector.astype(BF), tokens, preferred_element_type=F32).astype(BF)
    dy_rows = jnp.dot(scaled.astype(BF), out_grad, preferred_element_type=F32).astype(BF)
    xin = jnp.stack(
        [x_rows.reshape(E_WIN, CAP, feature_cols), dy_rows.reshape(E_WIN, CAP, feature_cols)], 1
    )
    rows, gate_grad, up_grad, down_grad = moe(xin, gate_weight, up_weight, down_weight)
    rows = rows.reshape(slot_rows, feature_cols + PROB)
    token_grad = lax.dot_general(
        selector,
        rows[:, :feature_cols],
        TN,
        precision=lax.Precision.HIGHEST,
        preferred_element_type=F32,
    ).astype(BF)
    summed_p = jnp.sum(rows[:, feature_cols:], axis=1)
    picked = jnp.sum(jnp.where(pick_map, summed_p[:, None, None], 0.0), axis=0)
    prob_grad = picked / probs.astype(F32)
    return (token_grad, prob_grad, gate_grad, up_grad, down_grad)


def solution(mesh):
    in_specs = (
        P("ep", "etp"),
        P("ep", "etp"),
        P("ep", None),
        P("ep", None),
        P("ep", None),
        P("ep", None),
        P("etp", "ep"),
        P("etp", "ep"),
        P("ep", "etp"),
    )
    out_specs = (P("ep", "etp"), P("ep", None), P("etp", "ep"), P("etp", "ep"), P("ep", "etp"))
    return jax.shard_map(shards, mesh=mesh, in_specs=in_specs, out_specs=out_specs, check_vma=False)
```

time: 641 us -> 148 us (0.23)
  waiting for transfers between devices: 513 us -> 0 us
  Pallas kernels: 0 us -> 134 us
  starting transfers between devices: 38.2 us -> 0 us
  matrix products: 36.2 us -> 2.96 us
  between operations: 14.2 us -> 0.73 us
  blocking collectives: 13.2 us -> 0 us
  other arithmetic: 12.8 us -> 3.82 us
  local copies, waits for them, and re-layouts: 12.4 us -> 5 us
    all_to_all x4 -> x0, waiting for transfers between devices: 399 us -> none  [the longest x1 141 us: shards(): lax.all_to_all(x_send, 'ep', split_axis=0, concat_axis=0, tiled=True)]
    pallas_call x0 -> x1, Pallas kernels: none -> 134 us  [moe(): pl.pallas_call(moe_kernel, out_shape=(jax.ShapeDtypeStruct((E_WIN, CAP, w...]
    psum x1 -> x0, waiting for transfers between devices: 114 us -> none  [shards(): summed = lax.psum(jnp.concatenate([forward, backward], 1), 'etp')]
    all_to_all x4 -> x0, starting transfers between devices: 38.1 us -> none  [the longest x1 12.3 us: shards(): lax.all_to_all(x_send, 'ep', split_axis=0, concat_axis=0, tiled=True)]
    dot_general x10 -> x3, matrix products: 36.2 us -> 2.96 us  [the longest x1 2.57 us: shards(): lax.dot_general(selector, rows[:, :feature_cols], TN, precision=lax.Preci...]
    all_to_all x1 -> x0, blocking collectives: 13.2 us -> none  [shards(): lax.all_to_all(p_send, 'ep', split_axis=0, concat_axis=0, tiled=True)]
    broadcast_in_dim x3 -> x0, local copies, waits for them, and re-layouts: 6.91 us -> none  [the longest x1 3.43 us: shards(): x_send = jnp.repeat(x_blocks, groups, axis=0)]
  transfers between devices with their start and end apart: 5 -> 0, of which waited for: 5 -> 0; matrix products, arithmetic and copies ran while one was open for 5% -> 0% of each run, Pallas kernels for 0% -> 0%
where the time goes in v1:
time: 148 us; the launch traced here: 146 us
  Pallas kernels  134 us (91%)
  local copies, waits for them, and re-layouts  5 us (3%)
  other arithmetic  3.82 us (3%)
  matrix products  2.96 us (2%)
    pallas_call x1, Pallas kernels, moe(): pl.pallas_call(moe_kernel, out_shape=(jax.ShapeDtypeStruct((E_WIN, CAP, w...  134 us
    unnamed x19, local copies, waits for them, and re-layouts  5 us

profile of v1, /device:TPU:6, one launch (start us, length us, event | category | flops | bytes accessed | tf_op | source)
XLA Modules:
  0.0 146.4 jit_solution(15649063516815648659)
XLA Ops:
  0.6 0.0 copy-start
  0.6 0.0 copy-start.5
  0.7 0.0 copy-start.6
  0.7 0.0 copy-start.4
  0.7 0.7 copy-done.5
  1.4 0.0 copy-done.6
  1.4 0.1 select_reduce_fusion.2
  1.5 0.7 and_select_fusion
  2.1 0.7 convert_element_type.25
  2.8 0.0 copy-done
  2.8 0.2 convolution_convert_fusion.1
  3.0 0.0 copy-done.4
  3.0 0.2 convolution_convert_fusion.2
  3.2 0.8 pad_maximum_fusion.xin
  4.0 133.9 %shard_map.128 = (f32[2,32,1664]{2,1,0:T(8,128)}, bf16[1536,256]{1,0:T(8,128)(2,1)}, bf16[1536,256]{1,0:T(8,128)(2,1)}, bf16[256,1536]{1,0:T(8,128)(2,1)}) custom-call(bf16[2,2,32,1536]{3,2,1,0:T(8,128)(2,1)} %pad_maximum_fusion.xin, bf16[1536,256]{1,0:T(8,128)(2,1)} %wg_hbm.1, bf16[1536,256]{1,0:T(8,128)(2,1)} %wu_hbm.1, bf16[256,1536]{1,0:T(8,128)(2,1)} %wd_hbm.1), custom_call_target="tpu_custom_call" | custom-call | flops 12999999488 | bytes 8000000 | tf_op jit(solution)/shard_map/pallas_call | solution.py:373
  138.0 0.0 copy-start.3
  138.0 0.9 slice_reduce_fusion
  138.9 2.6 %convolution_convert_fusion = bf16[128,1536]{1,0:T(8,128)(2,1)} fusion(f32[64,128]{1,0:T(8,128)S(1)} %get-tuple-element.14, f32[64,1664]{1,0:T(8,128)} %bitcast.11), kind=kOutput, calls=%fused_computation | convolution fusion | flops 151191552 | bytes 819200 | tf_op jit(solution)/shard_map/dot_general | solution.py:438
  141.5 0.0 copy-start.7
  141.5 0.1 select_reduce_fusion
  141.6 0.6 copy-done.7
  142.2 0.6 convert_divide_fusion
  142.7 0.0 copy-done.3
  142.7 0.0 copy-start.2
  142.7 0.9 copy.20
  143.6 0.5 copy-done.2
  144.2 0.0 copy-start.1
  144.2 0.9 copy.21
  145.0 0.5 copy-done.1
  145.6 0.9 copy.22
  (1 shorter events, 0.0 us)
Async XLA Ops:
  0.6 2.2 %copy-start = (bf16[128,1536]{1,0:T(8,128)(2,1)S(1)}, bf16[128,1536]{1,0:T(8,128)(2,1)}, u32[]{:S(2)}) copy-start(bf16[128,1536]{1,0:T(8,128)(2,1)} %param.10) | copy-start | bytes 1179652
  0.6 0.7 copy-start.5
  0.7 0.7 copy-start.6
  0.7 2.4 %copy-start.4 = (bf16[128,1536]{1,0:T(8,128)(2,1)S(1)}, bf16[128,1536]{1,0:T(8,128)(2,1)}, u32[]{:S(2)}) copy-start(bf16[128,1536]{1,0:T(8,128)(2,1)} %param.9) | copy-start | bytes 1179652
  138.0 4.8 %copy-start.3 = (bf16[1536,256]{1,0:T(8,128)(2,1)S(1)}, bf16[1536,256]{1,0:T(8,128)(2,1)}, u32[]{:S(2)}) copy-start(bf16[1536,256]{1,0:T(8,128)(2,1)} %get-tuple-element.22) | copy-start | bytes 2359300
  141.5 0.7 copy-start.7
  142.7 1.4 copy-start.2
  144.2 1.4 copy-start.1
